TPU v7x, 256 devices: a whole 4x4x8 slice. The times are simulated.
256 devices in a mesh: wide: 16 (over y, z_hi, core), expert: 16 (over z_lo, x).
Axes of the slice: x: 4, y: 4, z: 8 (z_hi: 2, z_lo: 4; z = z_hi * 4 + z_lo), core: 2. Of those that a mesh axis runs over, the one named last changes fastest.
Arguments:
- prompt: bfloat16 [2048, 4096], P('expert'), may hold values from -6 to 6
- steer_vec: float32 [4096], replicated, may hold values from -6 to 6
- strengths: float32 [16], P('wide'), may hold values from -2 to 2
- norm_gain: float32 [4096], replicated, may hold values from 0.25 to 1.75
- expert_ids: int32 [2048, 8], P('expert'), may hold values from 0 to 15, all different within a row; in each aligned block of 128 rows (0 to 127, 128 to 255, ...) at most 72 rows name the same one
- gate_values: float32 [2048, 8], P('expert'), may hold values from 0.02 to 0.5
- up_weight: bfloat16 [16, 4096, 768], P('expert', 'wide'), may hold values from -0.09375 to 0.09375
- down_weight: bfloat16 [16, 768, 4096], P('expert', None, 'wide'), may hold values from -0.21875 to 0.21875
Outputs:
- mixed: bfloat16 [16, 2048, 4096], P('wide', 'expert')
Inputs may be any that keep to these rules, and one draw needn't show every extreme that they name: `expert_ids`: each row names 8 different experts. Among the rows of one device of expert (aligned blocks of 128 rows) no expert is named more than 72 times, and in every draw some expert is named exactly 72 times in some block.
All inputs are finite; a program needn't handle non-finite values.
Results may differ from a plain program's by a relative error of at most 0.0065.
Values may be sent and summed in bfloat16 or wider, within the bound.
A program may use at most 128 MiB of HBM per device.

v0:
```python
import jax
import jax.numpy as jnp
from jax import lax
from jax.sharding import PartitionSpec as P

D = 4096


epsilon = 1e-06


def steer_rows(rows, strength, steer_vec, norm_gain):
    shifted = rows.astype(jnp.float32) + strength * steer_vec
    mean_square = jnp.mean(shifted * shifted, axis=-1, keepdims=True)
    return (shifted * lax.rsqrt(mean_square + epsilon) * norm_gain).astype(jnp.bfloat16)


def local(prompt, steer_vec, strengths, norm_gain, expert_ids, gate_values, up_weight, down_weight):
    tok_rows = prompt.shape[0]
    chosen_count = expert_ids.shape[1]
    experts = lax.axis_size("expert")
    capacity = min(tok_rows, tok_rows * chosen_count * 9 // (8 * experts))
    flat_ids = expert_ids.reshape(-1)
    onehot = (flat_ids[:, None] == jnp.arange(experts, dtype=jnp.int32)[None, :]).astype(jnp.int32)
    earlier = jnp.cumsum(onehot, axis=0) - onehot
    slot_index = jnp.sum(earlier * onehot, axis=1)
    dest_rows = flat_ids * capacity + slot_index
    token_of = jnp.arange(tok_rows * chosen_count, dtype=jnp.int32) // chosen_count
    source_rows = jnp.full((experts * capacity,), tok_rows, jnp.int32).at[dest_rows].set(token_of)
    strength = strengths[0]
    normed = steer_rows(prompt, strength, steer_vec, norm_gain)
    padded = jnp.concatenate([normed, jnp.zeros((1, D), jnp.bfloat16)], axis=0)
    outgoing = padded[source_rows].reshape(experts, capacity, D)
    incoming = lax.all_to_all(outgoing, "expert", split_axis=0, concat_axis=0, tiled=True)
    expert_rows = incoming.reshape(experts * capacity, D)
    upper = jnp.dot(
        expert_rows,
        lax.all_gather(up_weight, "wide", axis=1, tiled=True)[0],
        preferred_element_type=jnp.float32,
    )
    hidden = jax.nn.silu(upper).astype(jnp.bfloat16)
    outputs = jnp.dot(
        hidden,
        lax.all_gather(down_weight, "wide", axis=2, tiled=True)[0],
        preferred_element_type=jnp.float32,
    ).astype(jnp.bfloat16)
    returned_rows = lax.all_to_all(
        outputs.reshape(experts, capacity, D), "expert", split_axis=0, concat_axis=0, tiled=True
    )
    picked = returned_rows.reshape(experts * capacity, D)[dest_rows].reshape(
        tok_rows, chosen_count, D
    )
    result = jnp.sum(gate_values[:, :, None] * picked.astype(jnp.float32), axis=1)
    return result.astype(jnp.bfloat16)[None]


def solution(mesh):
    return jax.shard_map(
        local,
        mesh=mesh,
        in_specs=(
            P("expert", None),
            P(),
            P("wide"),
            P(),
            P("expert", None),
            P("expert", None),
            P("expert", "wide", None),
            P("expert", None, "wide"),
        ),
        out_specs=P("wide", "expert", None),
        check_vma=False,
    )
```

profile of v0, /device:TPU:80, one launch (start us, length us, event | category | flops | bytes accessed | tf_op | source)
XLA Modules:
  0.0 595.3 jit_solution(18281896074732338565)
XLA Ops:
  6.5 0.0 all-gather.3.cloned.1.call-start
  6.5 0.7 all-gather.3.cloned.1.call-update
  7.3 0.8 copy.14
  8.0 0.1 eq.29
  8.1 0.1 eq.25
  8.2 4.5 reduce-window.6
  12.8 0.1 slice.12
  12.8 0.1 copy.16
  13.0 0.1 copy.17
  13.1 0.7 broadcast_multiply_fusion.1
  13.8 0.1 copy.13
  13.9 0.1 mul.66
  14.6 0.7 broadcast_multiply_fusion
  15.4 1.6 multiply_reduce_fusion
  16.9 1.6 multiply_convert_fusion.1
  18.5 0.1 concatenate.3
  18.6 0.1 broadcast_add_fusion
  18.8 4.3 scatter_custom_fusion
  23.1 8.0 %gather_fusion = bf16[1152,4096]{1,0:T(8,128)(2,1)} fusion(bf16[129,4096]{1,0:T(8,128)(2,1)S(1)} %concatenate.3, s32[2048]{0:T(1024)S(1)} %pad_clamp_fusion), kind=kCustom, calls=%fused_computation | custom fusion | bytes 18878976 | tf_op jit(solution)/shard_map/gather | solution.py:33
  31.2 8.0 %all-to-all-start = ((bf16[16,72,4096]{2,1,0:T(8,128)(2,1)}), bf16[16,72,4096]{2,1,0:T(8,128)(2,1)}, u32[]{:S(2)}, u32[]{:S(2)}) async-start(bf16[16,72,4096]{2,1,0:T(8,128)(2,1)} %bitcast.42), calls=%async_computation | async-start | bytes 18874368 | tf_op jit(solution)/shard_map/all_to_all | solution.py:34
  39.2 0.0 all-gather.5.cloned.1.call-start
  39.2 0.7 all-gather.5.cloned.1.call-update
  39.9 79.3 %all-gather.3.cloned.1.call-done = bf16[1,4096,768]{2,1,0:T(8,128)(2,1)} async-done(((bf16[1,256,768]{2,1,0:T(8,128)(2,1)}), bf16[1,4096,768]{2,1,0:T(8,128)(2,1)}) %all-gather.3.cloned.1.call-update) | async-done | bytes 6291472 | tf_op jit(solution)/shard_map/all_gather | solution.py:38
  119.3 201.5 %all-to-all-done = bf16[16,72,4096]{2,1,0:T(8,128)(2,1)} async-done(((bf16[16,72,4096]{2,1,0:T(8,128)(2,1)}), bf16[16,72,4096]{2,1,0:T(8,128)(2,1)}, u32[]{:S(2)}, u32[]{:S(2)}) %all-to-all-start) | async-done | bytes 9437216 | tf_op jit(solution)/shard_map/all_to_all | solution.py:34
  320.7 12.2 %multiply_convert_fusion = bf16[1152,768]{1,0:T(8,128)(2,1)S(1)} fusion(bf16[1152,4096]{1,0:T(8,128)(2,1)} %bitcast.6, bf16[1,4096,768]{2,1,0:T(8,128)(2,1)} %all-gather.3.cloned.1.call-done), kind=kOutput, calls=%fused_computation.9 | convolution fusion | flops 7252180992 | bytes 17498112 | tf_op jit(solution)/shard_map/dot_general | solution.py:36
  332.9 0.0 all-gather.5.cloned.1.call-done
  333.0 12.5 %convolution_convert_fusion = bf16[1152,4096]{1,0:T(8,128)(2,1)} fusion(bf16[1152,768]{1,0:T(8,128)(2,1)S(1)} %multiply_convert_fusion, bf16[1,768,4096]{2,1,0:T(8,128)(2,1)} %all-gather.5.cloned.1.call-done), kind=kOutput, calls=%fused_computation.5 | convolution fusion | flops 7252475904 | bytes 17498112 | tf_op jit(solution)/shard_map/dot_general | solution.py:42
  345.5 0.0 copy-start
  345.5 5.2 all-to-all-start.1
  350.7 0.0 copy-done
  350.7 0.1 copy.12
  350.8 204.8 %all-to-all-done.1 = bf16[16,72,4096]{2,1,0:T(8,128)(2,1)} async-done(((bf16[16,72,4096]{2,1,0:T(8,128)(2,1)}), bf16[16,72,4096]{2,1,0:T(8,128)(2,1)}, u32[]{:S(2)}, u32[]{:S(2)}) %all-to-all-start.1) | async-done | bytes 9437216 | tf_op jit(solution)/shard_map/all_to_all | solution.py:47
  555.6 20.0 %gather_fusion.1 = bf16[1024,4096]{1,0:T(8,128)(2,1)} fusion(bf16[1152,4096]{1,0:T(8,128)(2,1)} %bitcast.10, s32[1024]{0:T(1024)S(1)} %broadcast_clamp_fusion), kind=kCustom, calls=%fused_computation.1 | custom fusion | bytes 16781312 | tf_op jit(solution)/shard_map/gather | solution.py:50
  575.6 12.9 %fusion = bf16[128,4096]{1,0:T(8,128)(2,1)} fusion(bf16[1024,4096]{1,0:T(8,128)(2,1)} %gather_fusion.1, f32[128,8]{1,0:T(8,128)S(1)} %copy.12), kind=kLoop, calls=%fused_computation.4 | loop fusion | flops 12058624 | bytes 9441280 | tf_op jit(solution)/shard_map/reduce_sum | solution.py:53
  (10 shorter events, 0.1 us)
Async XLA Ops:
  6.5 112.7 %all-gather.3.cloned.1.call-start = ((), (), s32[]{:S(2)}) async-start(), calls=%async_computation.2 | async-start | bytes 6684672 | tf_op jit(solution)/shard_map/all_gather | solution.py:38
  31.2 289.6 %all-to-all-start = ((bf16[16,72,4096]{2,1,0:T(8,128)(2,1)}), bf16[16,72,4096]{2,1,0:T(8,128)(2,1)}, u32[]{:S(2)}, u32[]{:S(2)}) async-start(bf16[16,72,4096]{2,1,0:T(8,128)(2,1)} %bitcast.42), calls=%async_computation | async-start | bytes 18874368 | tf_op jit(solution)/shard_map/all_to_all | solution.py:34
  39.2 293.8 %all-gather.5.cloned.1.call-start = ((), (), s32[]{:S(2)}) async-start(), calls=%async_computation.3 | async-start | bytes 6684672 | tf_op jit(solution)/shard_map/all_gather | solution.py:44
  345.5 5.3 copy-start
  345.5 210.1 %all-to-all-start.1 = ((bf16[16,72,4096]{2,1,0:T(8,128)(2,1)}), bf16[16,72,4096]{2,1,0:T(8,128)(2,1)}, u32[]{:S(2)}, u32[]{:S(2)}) async-start(bf16[16,72,4096]{2,1,0:T(8,128)(2,1)} %bitcast.43), calls=%async_computation.1 | async-start | bytes 18874368 | tf_op jit(solution)/shard_map/all_to_all | solution.py:47
Sparse Core Ops, SparseCore 0:
  10.0 109.1 all-gather.2
  121.8 118.2 all-gather.4
where the time goes:
time: 596 us; the launch traced here: 595 us
  waiting for transfers between devices  487 us (82%)
  local copies, waits for them, and re-layouts  34 us (6%)
  matrix products  24.7 us (4%)
  other arithmetic  22.2 us (4%)
  between operations  14.2 us (2%)
  starting transfers between devices  13.3 us (2%)
    all_to_all x1, waiting for transfers between devices, local(): lax.all_to_all(outputs.reshape(experts, capacity, D), 'expert', split_axi...  205 us
    all_to_all x1, waiting for transfers between devices, local(): lax.all_to_all(outgoing, 'expert', split_axis=0, concat_axis=0, tiled=True)  201 us
    all_gather x1, waiting for transfers between devices, local(): lax.all_gather(up_weight, 'wide', axis=1, tiled=True)[0]  79.3 us
    gather x1, local copies, waits for them, and re-layouts, local(): returned_rows.reshape(experts * capacity, D)[dest_rows]  20 us
    reduce_sum x1, other arithmetic, local(): jnp.sum(gate_values[:, :, None] * picked.astype(jnp.float32), axis=1)  12.9 us
    dot_general x1, matrix products, local(): jnp.dot(hidden, lax.all_gather(down_weight, 'wide', axis=2, tiled=True)[0...  12.5 us
    dot_general x1, matrix products, local(): jnp.dot(expert_rows, lax.all_gather(up_weight, 'wide', axis=1, tiled=True...  12.2 us
  transfers between devices with their start and end apart: 4, of which 3 were waited for; matrix products, arithmetic and copies ran while one was open for 6% of the time, Pallas kernels for 0%

commit v1 on v0

v1 whole, which is shorter than its diff:
```python
import jax
import jax.numpy as jnp
from jax import lax
from jax.sharding import Mesh, PartitionSpec as P

D = 4096
EH = 768
epsilon = 1e-06

WIDE = ("y", "zh", "c")
EXPERT = ("zl", "x")


def local(prompt, steer_vec, strengths, norm_gain, expert_ids, gate_values, up_weight, down_weight):
    w = lax.axis_index(WIDE)
    x = lax.axis_index("x")
    rows = prompt.astype(jnp.float32)
    scaled = (rows * norm_gain).astype(jnp.bfloat16)
    part = lax.dynamic_slice(scaled, (0, w * 256), (128, 256))
    part = lax.all_gather(part, EXPERT, axis=0, tiled=True)
    upper = jnp.dot(part, up_weight[0], preferred_element_type=jnp.float32)
    upper = upper.astype(jnp.bfloat16).reshape(4, 4, 16, 8, EH).transpose(2, 0, 1, 3, 4)
    upper = lax.all_to_all(upper, WIDE, split_axis=0, concat_axis=0, tiled=True)
    upper = jnp.sum(upper.astype(jnp.float32), axis=0).astype(jnp.bfloat16)
    upper = lax.all_to_all(upper, "zl", split_axis=0, concat_axis=0, tiled=True)
    upper = lax.all_gather(upper, WIDE, axis=0)
    upper = upper.transpose(1, 2, 0, 3, 4).reshape(4, 512, EH)

    steer = lax.dynamic_slice(steer_vec * norm_gain, (w * 256,), (256,))
    high = steer.astype(jnp.bfloat16)
    low = (steer - high.astype(jnp.float32)).astype(jnp.bfloat16)
    push = jnp.dot(jnp.stack([high, low]), up_weight[0], preferred_element_type=jnp.float32)
    push = lax.psum(jnp.sum(push, axis=0), WIDE)
    push = lax.all_gather(push, "zl", axis=0)

    s4 = lax.all_gather(strengths[0], "y", axis=0)
    shifted = rows[None] + s4[:, None, None] * steer_vec
    inv = lax.rsqrt(jnp.mean(shifted * shifted, axis=-1) + epsilon)
    inv = lax.all_gather(inv, "x", axis=1, tiled=True)

    onehot = expert_ids[:, :, None] == jnp.arange(16, dtype=jnp.int32)
    gates = jnp.sum(jnp.where(onehot, gate_values[:, :, None], 0.0), axis=1)
    gates = lax.all_gather(gates, "x", axis=0, tiled=True).reshape(512, 4, 4)
    gates = lax.dynamic_index_in_dim(gates, x, axis=2, keepdims=False).T

    lower = lax.all_gather(down_weight[0], ("zh", "c", "zl"), axis=0)
    lower = lower.reshape(4, 4, EH, 256).transpose(1, 2, 0, 3).reshape(4 * EH, 1024)

    pre = upper[None].astype(jnp.float32) + s4[:, None, None, None] * push[None, :, None, :]
    hidden = jax.nn.silu(pre * inv[:, None, :, None]) * gates[None, :, :, None]
    hidden = hidden.astype(jnp.bfloat16).transpose(0, 2, 1, 3).reshape(4 * 512, 4 * EH)
    out = jnp.dot(hidden, lower, preferred_element_type=jnp.float32).astype(jnp.bfloat16)
    out = out.reshape(16, 128, 1024)
    out = lax.all_to_all(out, ("y", "x"), split_axis=0, concat_axis=0, tiled=True)
    out = jnp.sum(out.reshape(4, 4, 128, 1024).astype(jnp.float32), axis=1)
    return out.transpose(1, 0, 2).reshape(1, 128, D).astype(jnp.bfloat16)


def solution(mesh):
    fine = Mesh(mesh.devices.reshape(4, 2, 2, 4, 4), ("y", "zh", "c", "zl", "x"))
    return jax.shard_map(
        local,
        mesh=fine,
        in_specs=(
            P(EXPERT, None),
            P(),
            P(WIDE),
            P(),
            P(EXPERT, None),
            P(EXPERT, None),
            P(EXPERT, WIDE, None),
            P(EXPERT, None, WIDE),
        ),
        out_specs=P(WIDE, EXPERT, None),
        check_vma=False,
    )
```

time: 596 us -> 455 us (0.76)
  the two profiles are of different devices: /device:TPU:80 before, /device:TPU:16 now
where the time goes in v1:
time: 455 us; the launch traced here: 452 us
  blocking collectives  262 us (58%)
  waiting for transfers between devices  101 us (22%)
  other arithmetic  29.6 us (7%)
  local copies, waits for them, and re-layouts  27.5 us (6%)
  matrix products  18.3 us (4%)
  between operations  13.9 us (3%)
    all_to_all x1, blocking collectives, local(): upper = lax.all_to_all(upper, WIDE, split_axis=0, concat_axis=0, tiled=True)  104 us
    all_gather x1, waiting for transfers between devices, local(): part = lax.all_gather(part, EXPERT, axis=0, tiled=True)  83.2 us
    all_to_all x1, blocking collectives, local(): lax.all_to_all(out, ('y', 'x'), split_axis=0, concat_axis=0, tiled=True)  56.8 us
    psum x1, blocking collectives, local(): push = lax.psum(jnp.sum(push, axis=0), WIDE)  39.5 us
    convert_element_type x1, other arithmetic, local(): hidden.astype(jnp.bfloat16).transpose(0, 2, 1, 3).reshape(4 * 512, 4 * EH)  17.6 us
    all_to_all x1, blocking collectives, local(): upper = lax.all_to_all(upper, 'zl', split_axis=0, concat_axis=0, tiled=True)  17.5 us
    all_gather x1, waiting for transfers between devices, local(): upper = lax.all_gather(upper, WIDE, axis=0)  16.9 us
    dot_general x1, matrix products, local(): jnp.dot(hidden, lower, preferred_element_type=jnp.float32)  15.9 us
  transfers between devices with their start and end apart: 3, of which 2 were waited for; matrix products, arithmetic and copies ran while one was open for 5% of the time, Pallas kernels for 0%

profile of v1, /device:TPU:16, one launch (start us, length us, event | category | flops | bytes accessed | tf_op | source)
XLA Modules:
  0.0 452.4 jit_solution(12546167525667356901)
XLA Ops:
  6.5 0.0 copy-start
  6.5 0.0 all-gather.6.cloned.1.call-start
  6.5 1.5 convert_element_type.72
  8.0 0.0 copy-start.2
  8.0 1.5 subtract_convert_fusion
  9.5 0.6 fusion.2
  10.2 0.0 all-gather.6.cloned.1.call-update
  10.2 0.0 all-gather.8.cloned.1.call-start
  10.2 0.7 all-gather.8.cloned.1.call-update
  10.9 0.0 all-gather.10.cloned.1.call-start
  11.0 83.2 %all-gather.6.cloned.1.call-done = bf16[2048,256]{1,0:T(8,128)(2,1)} async-done(((bf16[128,256]{1,0:T(8,128)(2,1)}), bf16[2048,256]{1,0:T(8,128)(2,1)}) %all-gather.6.cloned.1.call-update) | async-done | bytes 1048592 | tf_op jit(solution)/shard_map/all_gather | solution.py:20
  94.2 0.0 copy-done
  94.2 2.2 convolution_convert_fusion.1
  96.4 0.4 copy.51
  96.8 0.0 copy-done.2
  96.8 0.0 copy-start.3
  96.8 103.7 %all_to_all.15 = bf16[16,4,4,8,768]{4,3,2,1,0:T(8,128)(2,1)S(1)} all-to-all(bf16[16,4,4,8,768]{4,3,2,1,0:T(8,128)(2,1)S(1)} %bitcast.45), channel_id=1, replica_groups=mesh['y'=4,'zh'=2,'c'=2,'zl'=4,'x'=4] {'y','zh','c'}, dimensions={0} | all-to-all | bytes 6291456 | tf_op jit(solution)/shard_map/all_to_all | solution.py:23
  200.5 1.3 reduce_sum.48
  201.8 17.5 %all_to_all.16 = bf16[4,4,8,768]{3,2,1,0:T(8,128)(2,1)} all-to-all(bf16[4,4,8,768]{3,2,1,0:T(8,128)(2,1)} %reduce_sum.48), channel_id=1, replica_groups=mesh['y'=4,'zh'=2,'c'=2,'zl'=4,'x'=4] {'zl'}, dimensions={0} | all-to-all | bytes 393216 | tf_op jit(solution)/shard_map/all_to_all | solution.py:25
  219.3 0.0 all-gather.10.cloned.1.call-update
  220.0 1.3 dynamic-slice
  221.2 0.8 dynamic-update-slice
  222.0 8.6 %all-reduce = f32[4]{0:T(128)S(1)} all-reduce(f32[4]{0:T(128)S(1)} %dynamic-update-slice), channel_id=1, replica_groups=mesh['y'=4,'zh'=2,'c'=2,'zl'=4,'x'=4] {'y'}, use_global_device_ids=true, to_apply=%add | all-reduce | flops 4 | bytes 32
  230.6 0.7 stack.10
  231.3 0.7 stack.9
  231.9 0.2 convolution_reduce_fusion
  232.1 39.5 %psum.7 = f32[1,768]{1,0:T(1,128)S(1)} all-reduce(f32[1,768]{1,0:T(1,128)S(1)} %all_gather.31), channel_id=1, replica_groups=mesh['y'=4,'zh'=2,'c'=2,'zl'=4,'x'=4] {'y','zh','c'}, use_global_device_ids=true, to_apply=%region_2.0 | all-reduce | flops 768 | bytes 6144 | tf_op jit(solution)/shard_map/psum | solution.py:33
  271.7 13.0 %all-gather.1 = f32[4,1,768]{2,1,0:T(1,128)S(1)} all-gather(f32[1,1,768]{2,1,0:T(1,128)S(1)} %bitcast.54), channel_id=1, replica_groups=mesh['y'=4,'zh'=2,'c'=2,'zl'=4,'x'=4] {'zl'}, dimensions={0}, use_global_device_ids=true | all-gather | bytes 15360 | tf_op jit(solution)/shard_map/all_gather | solution.py:34
  284.7 0.7 select_reduce_fusion
  285.4 12.5 %all_gather.34 = f32[512,16]{0,1:T(8,128)S(1)} all-gather(f32[128,16]{0,1:T(8,128)S(1)} %select_reduce_fusion), channel_id=1, replica_groups=mesh['y'=4,'zh'=2,'c'=2,'zl'=4,'x'=4] {'x'}, dimensions={0}, use_global_device_ids=true | all-gather | bytes 40960 | tf_op jit(solution)/shard_map/all_gather | solution.py:43
  298.0 0.1 copy.45
  298.1 0.0 copy-done.3
  298.1 0.1 broadcast_multiply_fusion
  298.2 2.5 multiply_reduce_fusion
  300.7 10.6 %all_gather.33 = f32[4,512]{1,0:T(4,128)S(1)} all-gather(f32[4,128]{1,0:T(4,128)S(1)} %add_rsqrt_fusion), channel_id=1, replica_groups=mesh['y'=4,'zh'=2,'c'=2,'zl'=4,'x'=4] {'x'}, dimensions={1}, use_global_device_ids=true | all-gather | bytes 10240 | tf_op jit(solution)/shard_map/all_gather | solution.py:39
  311.4 0.1 broadcast_multiply_fusion.1
  311.4 0.0 all-gather.8.cloned.1.call-done
  311.4 7.6 %copy.42 = bf16[4,4,768,256]{3,0,2,1:T(4,128)(2,1)S(1)} copy(bf16[4,4,768,256]{3,2,1,0:T(8,128)(2,1)} %bitcast.46) | data formatting | bytes 12582912 | tf_op jit(solution)/shard_map/reshape | solution.py:47
  319.1 4.7 %copy.48 = bf16[384,8,4,256]{3,1,2,0:T(8,128)(2,1)} copy(bf16[384,8,4,256]{3,2,1,0:T(4,128)(2,1)S(1)} %bitcast.42) | data formatting | bytes 12582912
  323.8 16.9 %all-gather.10.cloned.1.call-done = bf16[64,4,8,768]{3,2,1,0:T(8,128)(2,1)} async-done(((bf16[4,4,8,768]{3,2,1,0:T(8,128)(2,1)}), bf16[64,4,8,768]{3,2,1,0:T(8,128)(2,1)}) %all-gather.10.cloned.1.call-update) | async-done | bytes 3145744 | tf_op jit(solution)/shard_map/all_gather | solution.py:26
  340.7 2.7 convert_bitcast_fusion
  343.4 0.7 copy.39
  344.2 4.3 copy.40
  348.4 17.6 %multiply_convert_fusion = bf16[4,512,4,768]{3,2,1,0:T(4,128)(2,1)S(1)} fusion(f32[512,4]{1,0:T(8,128)S(1)} %bitcast.52, f32[4,512]{1,0:T(4,128)S(1)} %all_gather.33, f32[4,4,768]{2,1,0:T(4,128)S(1)} %broadcast_multiply_fusion.1, f32[512,4,768]{2,1,0:T(4,128)S(1)} %copy.40), kind=kLoop, calls=%fused_computation.1 | loop fusion | flops 50331648 | bytes 18939904 | tf_op jit(solution)/shard_map/convert_element_type | solution.py:51
  366.0 4.1 copy.47
  370.2 15.9 %convolution_convert_fusion = bf16[2048,1024]{1,0:T(8,128)(2,1)S(1)} fusion(bf16[2048,3072]{1,0:T(8,128)(2,1)S(1)} %bitcast.44, bf16[3072,1024]{1,0:T(8,128)(2,1)} %bitcast.47), kind=kOutput, calls=%fused_computation.5 | convolution fusion | flops 12886999040 | bytes 23068672 | tf_op jit(solution)/shard_map/dot_general | solution.py:52
  386.1 0.0 copy-start.1
  386.1 56.8 %all_to_all.17 = bf16[16,128,1024]{2,1,0:T(8,128)(2,1)S(1)} all-to-all(bf16[16,128,1024]{2,1,0:T(8,128)(2,1)S(1)} %bitcast.49), channel_id=1, replica_groups=mesh['y'=4,'zh'=2,'c'=2,'zl'=4,'x'=4] {'y','x'}, dimensions={0} | all-to-all | bytes 8388608 | tf_op jit(solution)/shard_map/all_to_all | solution.py:54
  442.9 1.0 bitcast_reduce_fusion
  443.8 0.7 copy.43
  444.5 1.3 copy.44
  445.8 0.0 copy-done.1
  (6 shorter events, 0.0 us)
Async XLA Ops:
  6.5 87.6 %copy-start = (bf16[1,256,768]{2,1,0:T(8,128)(2,1)S(1)}, bf16[1,256,768]{2,1,0:T(8,128)(2,1)}, u32[]{:S(2)}) copy-start(bf16[1,256,768]{2,1,0:T(8,128)(2,1)} %param.14) | copy-start | bytes 1179652
  6.5 87.6 %all-gather.6.cloned.1.call-start = ((), (), s32[]{:S(2)}) async-start(), calls=%async_computation.3 | async-start | bytes 1114112 | tf_op jit(solution)/shard_map/all_gather | solution.py:20
  8.0 88.8 %copy-start.2 = (f32[128,4096]{1,0:T(8,128)}, f32[128,4096]{1,0:T(8,128)S(1)}, u32[]{:S(2)}) copy-start(f32[128,4096]{1,0:T(8,128)S(1)} %convert_element_type.72) | copy-start | bytes 6291460
  10.2 301.3 %all-gather.8.cloned.1.call-start = ((), (), s32[]{:S(2)}) async-start(), calls=%async_computation.4 | async-start | bytes 6684672 | tf_op jit(solution)/shard_map/all_gather | solution.py:46
  10.9 329.7 %all-gather.10.cloned.1.call-start = ((), (), s32[]{:S(2)}) async-start(), calls=%async_computation.5 | async-start | bytes 3342336 | tf_op jit(solution)/shard_map/all_gather | solution.py:26
  96.8 201.3 %copy-start.3 = (f32[4096]{0:T(1024)S(1)}, f32[4096]{0:T(1024)}, u32[]{:S(2)}) copy-start(f32[4096]{0:T(1024)} %param.9) | copy-start | bytes 49156
  386.1 59.8 %copy-start.1 = (bf16[1,256,768]{2,1,0:T(8,128)(2,1)S(1)}, bf16[1,256,768]{2,1,0:T(8,128)(2,1)}, u32[]{:S(2)}) copy-start(bf16[1,256,768]{2,1,0:T(8,128)(2,1)} %param.14) | copy-start | bytes 1179652
Sparse Core Ops, SparseCore 0:
  10.3 83.8 all-gather.5
  96.0 176.4 all-gather.7
  275.2 65.4 all-gather.9

commit v2 on v1

v2 whole, which is shorter than its diff:
```python
import jax
import jax.numpy as jnp
from jax import lax
from jax.experimental import pallas as pl
from jax.experimental.pallas import tpu as pltpu
from jax.sharding import Mesh, PartitionSpec as P

D = 4096
EH = 768
epsilon = 1e-06

WIDE = ("y", "zh", "c")
EXPERT = ("zl", "x")
MESH = pl.DeviceIdType.MESH
F32 = jnp.float32
BF16 = jnp.bfloat16
TURN = (2, 1, 3, 0)


def kernel(
    prompt, steer, strength, gain, ids, gates, up, down, out,
    sbuf, pgb, misc, ub, db, psend, precv, upper, aown, ab, qb, hb, part, rsend, rrecv, msend, mrecv, fin,
    load_sem, s_snd, s_rcv, p_snd, p_rcv, m_snd, m_rcv, ring_snd, ring_rcv, sib_snd, sib_rcv,
    rs_snd, rs_rcv, ag_snd, ag_rcv, q_snd, q_rcv, rl_snd, rl_rcv, mn_snd, mn_rcv, f_snd, f_rcv, f_loc,
):
    y, zh, c = lax.axis_index("y"), lax.axis_index("zh"), lax.axis_index("c")
    zl, x = lax.axis_index("zl"), lax.axis_index("x")
    zz = zh * 4 + zl
    sib = 1 - c

    def at_z(step):
        z = lax.rem(zz + step + 8, 8)
        return z // 4, lax.rem(z, 4)

    def z_id(step):
        a, b = at_z(step)
        return {"zh": a, "zl": b}

    def x_id(d):
        return {"x": lax.rem(x + d, 4)}

    def yc_id(d, b):
        return {"y": lax.rem(y + d, 4), "c": lax.rem(c + b, 2)}

    def remote(src, dst, snd, rcv, dev):
        return pltpu.make_async_remote_copy(
            src_ref=src, dst_ref=dst, send_sem=snd, recv_sem=rcv, device_id=dev, device_id_type=MESH
        )

    def slot(t, step, core, half=None):
        a, b = at_z(step)
        if t == 0:
            if half is None:
                return ub.at[b, pl.ds((a * 2 + core) * 256, 256), :]
            return ub.at[b, pl.ds((a * 2 + core) * 256 + half * 128, 128), :]
        if half is None:
            return db.at[a, core, pl.ds(b * EH, EH), :]
        return db.at[a, core, pl.ds(b * EH + half * 384, 384), :]

    load = [
        pltpu.make_async_copy(up, slot(0, 0, c), load_sem.at[0]),
        pltpu.make_async_copy(down, slot(1, 0, c), load_sem.at[1]),
    ]
    for cp in load:
        cp.start()

    partners = [z_id(1), z_id(-1)] + [x_id(d) for d in (1, 2, 3)]
    partners += [yc_id(d, b) for d in range(4) for b in range(2) if d or b]
    barrier = pltpu.get_barrier_semaphore()
    for dev in partners:
        pl.semaphore_signal(barrier, inc=1, device_id=dev, device_id_type=MESH)
    pl.semaphore_wait(barrier, len(partners))

    def ring(t, way, k):
        sign = 1 if way == 0 else -1
        half = way if k == 4 else None
        piece = slot(t, -sign * (k - 1), c, half)
        return remote(piece, piece, ring_snd.at[t, way, k - 1], ring_rcv.at[t, way, k - 1], z_id(sign))

    def ring_send(t, k):
        for way in (0, 1):
            ring(t, way, k).start()

    def sibling(t, n):
        step = (0, -1, 1, -2, 2, -3, 3, 4)[n]
        piece = slot(t, step, c)
        return remote(piece, piece, sib_snd.at[t, n], sib_rcv.at[t, n], {"c": sib})

    def ring_take(t, k):
        for way in (0, 1):
            ring(t, way, k).wait_recv()
        if k < 4:
            ring_send(t, k + 1)
            sibling(t, 2 * k - 1).start()
            sibling(t, 2 * k).start()
        else:
            sibling(t, 7).start()

    load[0].wait()
    ring_send(0, 1)
    sibling(0, 0).start()

    me = y * 2 + c
    sbuf[me] = strength[...]
    others = [(d, b) for d in range(4) for b in range(2) if d or b]

    def strengths_copy(d, b):
        n = d * 2 + b
        return remote(sbuf.at[me], sbuf.at[me], s_snd.at[n], s_rcv.at[n], yc_id(d, b))

    for d, b in others:
        strengths_copy(d, b).start()

    rows = pl.ds(pl.multiple_of(c * 64, 64), 64)
    cols = pl.ds(pl.multiple_of(y * 1024, 1024), 1024)
    mine = pl.ds(pl.multiple_of(x * 64, 64), 64)
    pgb[mine, :] = (prompt[rows, cols].astype(F32) * gain[:, cols]).astype(BF16)

    def prompt_copy(d):
        return remote(pgb.at[mine, :], pgb.at[mine, :], p_snd.at[d], p_rcv.at[d], x_id(d))

    for d in (1, 2, 3):
        prompt_copy(d).start()
    steered = steer[:, cols] * gain[:, cols]
    high = steered.astype(BF16).astype(F32)
    which = lax.broadcasted_iota(jnp.int32, (16, 1024), 0)
    pgb[256:272, :] = jnp.where(which == 0, high, jnp.where(which == 1, steered - high, 0.0)).astype(BF16)

    load[1].wait()
    sibling(1, 0).start()
    ring_take(0, 1)

    for d, b in others:
        strengths_copy(d, b).wait()
    lane = lax.broadcasted_iota(jnp.int32, (64, 128), 1)
    table = jnp.zeros((64, 128), F32)
    for k in range(8):
        table = table + jnp.where(lane == ids[rows, k:k + 1], gates[rows, k:k + 1], 0.0)
    misc[x] = table

    @pl.loop(0, 8)
    def _(j):
        s = sbuf[j][0:1, 0:1]
        square = jnp.zeros((64, 1), F32)
        for n in range(8):
            piece = prompt[rows, n * 512:(n + 1) * 512].astype(F32) + s * steer[:, n * 512:(n + 1) * 512]
            square = square + jnp.sum(piece * piece, axis=1, keepdims=True)
        misc[x] = misc[x] + jnp.where(lane == 16 + j, lax.rsqrt(square * (1.0 / D) + epsilon), 0.0)

    def misc_copy(d):
        return remote(misc.at[x], misc.at[x], m_snd.at[d], m_rcv.at[d], x_id(d))

    for d in (1, 2, 3):
        misc_copy(d).start()

    def turn(i):
        return lax.rem(zl + TURN[i], 4)

    def scatter_copy(i, d):
        e = turn(i)
        return remote(
            psend.at[e, lax.rem(y + d, 4)], precv.at[e, y], rs_snd.at[i, d], rs_rcv.at[i, d], yc_id(d, 0)
        )

    def expert(i):
        for n in ((3, 4), (2, 5), (1, 6), (0, 7))[i]:
            sibling(0, n).wait_recv()
        e = turn(i)
        for n in range(3):
            third = slice(n * 256, (n + 1) * 256)
            upper[...] = jnp.dot(pgb[...], ub[e, :, third], preferred_element_type=F32)
            for block in range(4):
                psend[e, block, :, third] = upper[block * 64:(block + 1) * 64, :].astype(BF16)
            aown[e, :, third] = upper[pl.ds(pl.multiple_of(y * 64, 64), 64), :]
            push = upper[256:264, :]
            qb[y, e, :, third] = push[0:1] + push[1:2] + jnp.zeros((8, 256), F32)
        for d in (1, 2, 3):
            scatter_copy(i, d).start()

    def gather_copy(i, d):
        e = turn(i)
        return remote(ab.at[y, e], ab.at[y, e], ag_snd.at[i, d], ag_rcv.at[i, d], yc_id(d, 0))

    def add_up(i):
        e = turn(i)
        total = aown[e]
        for d in (1, 2, 3):
            scatter_copy(i, d).wait_recv()
            total = total + precv[e, lax.rem(y + 4 - d, 4)].astype(F32)
        ab[y, e] = total.astype(BF16)
        for d in (1, 2, 3):
            gather_copy(i, d).start()

    def push_copy(d):
        return remote(qb.at[y], qb.at[y], q_snd.at[d], q_rcv.at[d], yc_id(d, 0))

    ring_take(0, 2)
    for d in (1, 2, 3):
        prompt_copy(d).wait_recv()
    expert(0)
    ring_take(0, 3)
    ring_send(1, 1)
    expert(1)
    expert(2)
    add_up(0)
    ring_take(0, 4)
    expert(3)
    for d in (1, 2, 3):
        push_copy(d).start()
    ring_take(1, 1)
    add_up(1)
    add_up(2)
    add_up(3)
    for d in (1, 2, 3):
        push_copy(d).wait_recv()
        misc_copy(d).wait_recv()
    for i in range(4):
        for d in (1, 2, 3):
            gather_copy(i, d).wait_recv()

    def hidden(g):
        dest_y = lax.rem(y + g + 1, 4)

        @pl.loop(0, 16)
        def _(n):
            block, e = n // 4, lax.rem(n, 4)
            pre = ab[block, e].astype(F32)
            here = misc[block]
            gate = jnp.sum(jnp.where(lane == e * 4 + x, here, 0.0), axis=1, keepdims=True)
            push = qb[0, e][0:1] + qb[1, e][0:1] + qb[2, e][0:1] + qb[3, e][0:1]
            for b in range(2):
                j = dest_y * 2 + b
                inv = 0.5 * jnp.sum(jnp.where(lane == 16 + j, here, 0.0), axis=1, keepdims=True)
                half = (pre + sbuf[j][0:1, 0:1] * push) * inv
                value = (half * gate) * (1.0 + jnp.tanh(half))
                hb[g, pl.ds(pl.multiple_of(block * 128 + b * 64, 64), 64),
                   pl.ds(pl.multiple_of(e * EH, 128), EH)] = value.astype(BF16)

    for k in (2, 3, 4):
        hidden(k - 2)
        ring_take(1, k)
    hidden(3)
    for n in range(8):
        sibling(1, n).wait_recv()

    def relay(g, way):
        return remote(
            rsend.at[g, way], rrecv.at[g, way], rl_snd.at[g, way], rl_rcv.at[g, way], x_id(1 + 2 * way)
        )

    def main(g, way):
        return remote(
            msend.at[g, way], mrecv.at[g, way], mn_snd.at[g, way], mn_rcv.at[g, way], x_id(1 + 2 * way)
        )

    def final(g, b):
        return remote(
            fin.at[g, pl.ds(pl.multiple_of(lax.rem(c + b, 2) * 64, 64), 64), :],
            out.at[0, rows, cols], f_snd.at[g, b], f_rcv.at[g, b], yc_id(g + 1, b),
        )

    def final_local():
        return pltpu.make_async_copy(fin.at[3, rows, :], out.at[0, rows, cols], f_loc)

    @pl.loop(0, 6)
    def _(t):
        @pl.when(t < 4)
        def _():
            @pl.loop(0, 2)
            def _(way):
                @pl.loop(0, 2)
                def _(n):
                    sums = jnp.dot(hb[t], db[way, n], preferred_element_type=F32)
                    place = pl.ds(pl.multiple_of(way * 512 + n * 256, 256), 256)
                    for block in range(4):
                        part[t, block, :, place] = sums[block * 128:(block + 1) * 128]
                    rsend[t, way, :, pl.ds(pl.multiple_of(n * 256, 256), 256)] = (
                        part[t, lax.rem(x + 2, 4), :, place].astype(BF16)
                    )

                relay(t, way).start()

        @pl.when(jnp.logical_and(t >= 1, t < 5))
        def _():
            g = t - 1
            for way in (0, 1):
                relay(g, way).wait_recv()
                block = lax.rem(x + 1 + 2 * way, 4)
                same = slice(way * 512, way * 512 + 512)
                other = slice(512 - way * 512, 1024 - way * 512)
                msend[g, way, :, same] = (part[g, block, :, same] + rrecv[g, way].astype(F32)).astype(BF16)
                msend[g, way, :, other] = part[g, block, :, other].astype(BF16)
                main(g, way).start()

        @pl.when(t >= 2)
        def _():
            g = t - 2
            main(g, 0).wait_recv()
            main(g, 1).wait_recv()
            fin[g] = (part[g, x] + mrecv[g, 0].astype(F32) + mrecv[g, 1].astype(F32)).astype(BF16)
            final(g, 1).start()

            @pl.when(g < 3)
            def _():
                final(g, 0).start()

            @pl.when(g == 3)
            def _():
                final_local().start()

    for d in (1, 2, 3):
        prompt_copy(d).wait_send()
        misc_copy(d).wait_send()
        push_copy(d).wait_send()
        for i in range(4):
            scatter_copy(i, d).wait_send()
            gather_copy(i, d).wait_send()
    for t in (0, 1):
        for k in (1, 2, 3, 4):
            for way in (0, 1):
                ring(t, way, k).wait_send()
        for n in range(8):
            sibling(t, n).wait_send()
    for g in range(4):
        for way in (0, 1):
            relay(g, way).wait_send()
            main(g, way).wait_send()
            if (g, way) != (3, 0):
                final(g, way).wait()
    final_local().wait()


def local(prompt, steer_vec, strengths, norm_gain, expert_ids, gate_values, up_weight, down_weight):
    vmem = pl.BlockSpec(memory_space=pltpu.VMEM)
    away = pl.BlockSpec(memory_space=pl.ANY)
    dma = pltpu.SemaphoreType.DMA
    return pl.pallas_call(
        kernel,
        out_shape=jax.ShapeDtypeStruct((1, 128, D), BF16),
        in_specs=[vmem] * 6 + [away] * 2,
        out_specs=away,
        scratch_shapes=[
            pltpu.VMEM((8, 8, 128), F32),
            pltpu.VMEM((272, 1024), BF16),
            pltpu.VMEM((4, 64, 128), F32),
            pltpu.VMEM((4, 1024, EH), BF16),
            pltpu.VMEM((2, 2, 4 * EH, 256), BF16),
            pltpu.VMEM((4, 4, 64, EH), BF16),
            pltpu.VMEM((4, 4, 64, EH), BF16),
            pltpu.VMEM((272, 256), F32),
            pltpu.VMEM((4, 64, EH), F32),
            pltpu.VMEM((4, 4, 64, EH), BF16),
            pltpu.VMEM((4, 4, 8, EH), F32),
            pltpu.VMEM((4, 512, 4 * EH), BF16),
            pltpu.VMEM((4, 4, 128, 1024), F32),
            pltpu.VMEM((4, 2, 128, 512), BF16),
            pltpu.VMEM((4, 2, 128, 512), BF16),
            pltpu.VMEM((4, 2, 128, 1024), BF16),
            pltpu.VMEM((4, 2, 128, 1024), BF16),
            pltpu.VMEM((4, 128, 1024), BF16),
            dma((2,)),
            dma((8,)), dma((8,)),
            dma((4,)), dma((4,)),
            dma((4,)), dma((4,)),
            dma((2, 2, 4)), dma((2, 2, 4)),
            dma((2, 8)), dma((2, 8)),
            dma((4, 4)), dma((4, 4)),
            dma((4, 4)), dma((4, 4)),
            dma((4,)), dma((4,)),
            dma((4, 2)), dma((4, 2)),
            dma((4, 2)), dma((4, 2)),
            dma((4, 2)), dma((4, 2)),
            dma(()),
        ],
        compiler_params=pltpu.CompilerParams(
            collective_id=0, has_side_effects=True, vmem_limit_bytes=60 * 1024 * 1024
        ),
        cost_estimate=pl.CostEstimate(flops=18_000_000_000, bytes_accessed=3_000_000, transcendentals=6_300_000),
    )(
        prompt,
        steer_vec[None],
        jnp.broadcast_to(strengths, (8, 128)),
        norm_gain[None],
        expert_ids,
        gate_values,
        up_weight[0],
        down_weight[0],
    )


def solution(mesh):
    fine = Mesh(mesh.devices.reshape(4, 2, 2, 4, 4), ("y", "zh", "c", "zl", "x"))
    return jax.shard_map(
        local,
        mesh=fine,
        in_specs=(
            P(EXPERT, None),
            P(),
            P(WIDE),
            P(),
            P(EXPERT, None),
            P(EXPERT, None),
            P(EXPERT, WIDE, None),
            P(EXPERT, None, WIDE),
        ),
        out_specs=P(WIDE, EXPERT, None),
        check_vma=False,
    )
```

time: 455 us -> 152 us (0.33)
  blocking collectives: 262 us -> 0 us
  Pallas kernels: 0 us -> 145 us
  waiting for transfers between devices: 101 us -> 0 us
  other arithmetic: 29.6 us -> 0 us
  local copies, waits for them, and re-layouts: 27.5 us -> 4.43 us
  matrix products: 18.3 us -> 0 us
  between operations: 13.9 us -> 0.67 us
    all_to_all x3 -> x0, blocking collectives: 178 us -> none  [the longest x1 104 us: local(): upper = lax.all_to_all(upper, WIDE, split_axis=0, concat_axis=0, tiled=True)]
    pallas_call x0 -> x1, Pallas kernels: none -> 145 us  [local(): pl.pallas_call(kernel, out_shape=jax.ShapeDtypeStruct((1, 128, D), BF16),...]
    all_gather x3 -> x0, waiting for transfers between devices: 100 us -> none  [the longest x1 83.2 us: local(): part = lax.all_gather(part, EXPERT, axis=0, tiled=True)]
    psum x1 -> x0, blocking collectives: 39.5 us -> none  [local(): push = lax.psum(jnp.sum(push, axis=0), WIDE)]
    all_gather x3 -> x0, blocking collectives: 36.2 us -> none  [the longest x1 13 us: local(): push = lax.all_gather(push, 'zl', axis=0)]
    convert_element_type x4 -> x0, other arithmetic: 21.2 us -> none  [the longest x1 17.6 us: local(): hidden.astype(jnp.bfloat16).transpose(0, 2, 1, 3).reshape(4 * 512, 4 * EH)]
    dot_general x3 -> x0, matrix products: 18.3 us -> none  [the longest x1 15.9 us: local(): jnp.dot(hidden, lower, preferred_element_type=jnp.float32)]
    unnamed x1 -> x0, blocking collectives: 8.59 us -> none
  transfers between devices with their start and end apart: 3 -> 0, of which waited for: 2 -> 0; matrix products, arithmetic and copies ran while one was open for 5% -> 0% of each run, Pallas kernels for 0% -> 0%
where the time goes in v2:
time: 152 us; the launch traced here: 150 us
  Pallas kernels  145 us (95%)
  local copies, waits for them, and re-layouts  4.43 us (3%)
    pallas_call x1, Pallas kernels, local(): pl.pallas_call(kernel, out_shape=jax.ShapeDtypeStruct((1, 128, D), BF16),...  145 us
    unnamed x7, local copies, waits for them, and re-layouts  3.84 us

profile of v2, /device:TPU:16, one launch (start us, length us, event | category | flops | bytes accessed | tf_op | source)
XLA Modules:
  0.0 150.3 jit_solution(15959215329095446067)
XLA Ops:
  0.7 0.0 copy-start
  0.7 0.6 broadcast_in_dim.12.strength
  1.3 0.1 copy-done
  1.3 0.0 copy-start.1
  1.3 0.7 copy.9.ids
  2.1 0.0 copy-done.1
  2.1 0.7 copy.10.gates
  2.8 145.2 %shard_map.85 = bf16[1,128,4096]{2,1,0:T(8,128)(2,1)} custom-call(bf16[128,4096]{1,0:T(8,128)(2,1)} %prompt.1, f32[1,4096]{1,0:T(1,128)} %bitcast.8, f32[8,128]{1,0:T(8,128)} %broadcast_in_dim.12.strength, f32[1,4096]{1,0:T(1,128)} %bitcast.9, s32[128,8]{1,0:T(8,128)} %copy.9.ids, f32[128,8]{1,0:T(8,128)} %copy.10.gates, bf16[256,768]{1,0:T(8,128)(2,1)} %bitcast.6, ...), custom_call_target="tpu_custom_call" | custom-call | flops 17999998976 | bytes 3000000 | tf_op jit(solution)/shard_map/pallas_call | solution.py:337
  148.0 2.3 %copy.13 = bf16[1,128,4096]{2,1,0:T(8,128)(2,1)} copy(bf16[1,128,4096]{2,1,0:T(8,128)(2,1)} %shard_map.85) | data formatting | bytes 2097152
Async XLA Ops:
  0.7 0.7 copy-start
  1.3 0.7 copy-start.1

commit v3 on v2

v3 whole, which is shorter than its diff:
```python
import jax
import jax.numpy as jnp
from jax import lax
from jax.experimental import pallas as pl
from jax.experimental.pallas import tpu as pltpu
from jax.sharding import Mesh, PartitionSpec as P

D = 4096
EH = 768
epsilon = 1e-06

WIDE = ("y", "zh", "c")
EXPERT = ("zl", "x")
MESH = pl.DeviceIdType.MESH
F32 = jnp.float32
BF16 = jnp.bfloat16
TURN = (2, 1, 3, 0)


def kernel(
    prompt, steer, strength, gain, ids, gates, up, down, out,
    sbuf, by_row, pgb, misc, gt, it, sq, ub, db, ab, qb, hb, part, rsend, rrecv, msend, mrecv, fin,
    load_sem, s_snd, s_rcv, p_snd, p_rcv, m_snd, m_rcv, ring_snd, ring_rcv, sib_snd, sib_rcv,
    a_snd, a_rcv, a_loc, ag_snd, ag_rcv, q_snd, q_rcv, rl_snd, rl_rcv, mn_snd, mn_rcv, f_snd, f_rcv, f_loc,
):
    y, zh, c = lax.axis_index("y"), lax.axis_index("zh"), lax.axis_index("c")
    zl, x = lax.axis_index("zl"), lax.axis_index("x")
    zz = zh * 4 + zl
    sib = 1 - c

    def at_z(step):
        z = lax.rem(zz + step + 8, 8)
        return z // 4, lax.rem(z, 4)

    def z_id(step):
        a, b = at_z(step)
        return {"zh": a, "zl": b}

    def x_id(d):
        return {"x": lax.rem(x + d, 4)}

    def yc_id(d, b):
        return {"y": lax.rem(y + d, 4), "c": lax.rem(c + b, 2)}

    def remote(src, dst, snd, rcv, dev):
        return pltpu.make_async_remote_copy(
            src_ref=src, dst_ref=dst, send_sem=snd, recv_sem=rcv, device_id=dev, device_id_type=MESH
        )

    def column(at_y, e):
        return lax.rem(at_y - e + 8, 4)

    def slot(p, step, core, h):
        a, b = at_z(step)
        if p == 0:
            return ub.at[b, pl.ds(2 * h, 2), a, core]
        return db.at[p - 1, a, pl.ds(pl.multiple_of(b * EH + h * 384, 128), 384),
                     pl.ds(pl.multiple_of(core * 128, 128), 128)]

    def held(p, step, fn):
        if p:
            fn()
        else:
            pl.when(column(y, at_z(step)[1]) < 3)(fn)

    load = [None]
    for p in (0, 1):
        load.append(pltpu.make_async_copy(
            down.at[:, p * 128:(p + 1) * 128],
            db.at[p, zh, pl.ds(pl.multiple_of(zl * EH, 128), EH), pl.ds(pl.multiple_of(c * 128, 128), 128)],
            load_sem.at[1 + p],
        ))
    for cp in load[1:]:
        cp.start()

    partners = [z_id(1), z_id(-1)] + [x_id(d) for d in (1, 2, 3)]
    partners += [yc_id(d, b) for d in range(4) for b in range(2) if d or b]
    barrier = pltpu.get_barrier_semaphore()
    for dev in partners:
        pl.semaphore_signal(barrier, inc=1, device_id=dev, device_id_type=MESH)
    pl.semaphore_wait(barrier, len(partners))

    def ring(p, h, way, k):
        sign = 1 if way == 0 else -1
        piece = slot(p, -sign * (k - 1), c, h)
        return remote(piece, piece, ring_snd.at[p, h, way, k - 1], ring_rcv.at[p, h, way, k - 1], z_id(sign))

    def ways(h, k):
        return (0, 1) if k < 4 else (h,)

    def ring_send(p, h, k):
        for way in ways(h, k):
            held(p, (k - 1) * (2 * way - 1), ring(p, h, way, k).start)

    def sibling_step(n):
        return (0, -1, 1, -2, 2, -3, 3, 4)[n]

    def sibling(p, h, n):
        piece = slot(p, sibling_step(n), c, h)
        return remote(piece, piece, sib_snd.at[p, h, n], sib_rcv.at[p, h, n], {"c": sib})

    def sibling_send(p, h, n):
        held(p, sibling_step(n), sibling(p, h, n).start)

    def ring_take(p, k):
        for h in (0, 1):
            for way in ways(h, k):
                held(p, k * (2 * way - 1), ring(p, h, way, k).wait_recv)
            if k < 4:
                ring_send(p, h, k + 1)
                sibling_send(p, h, 2 * k - 1)
                sibling_send(p, h, 2 * k)
            else:
                sibling_send(p, h, 7)

    def columns_copy(d):
        b = lax.rem(column(y + d, zl), 3)
        return remote(
            up.at[:, pl.ds(pl.multiple_of(b * 256, 256), 256)], ub.at[zl, y, zh, c],
            a_snd.at[d], a_rcv.at[d], yc_id(d, 0),
        )

    def columns_own():
        b = lax.rem(column(y, zl), 3)
        return pltpu.make_async_copy(
            up.at[:, pl.ds(pl.multiple_of(b * 256, 256), 256)], ub.at[zl, y, zh, c], a_loc
        )

    held(0, 0, columns_own().start)
    for d in (1, 2, 3):
        pl.when(column(y + d, zl) < 3)(columns_copy(d).start)
    load[1].wait()
    for h in (0, 1):
        ring_send(1, h, 1)

    me = y * 2 + c
    sbuf[me] = jnp.full((8, 128), strength[0], F32)
    others = [(d, b) for d in range(4) for b in range(2) if d or b]

    def strengths_copy(d, b):
        n = d * 2 + b
        return remote(sbuf.at[me], sbuf.at[me], s_snd.at[n], s_rcv.at[n], yc_id(d, b))

    for d, b in others:
        strengths_copy(d, b).start()

    rows = pl.ds(pl.multiple_of(c * 64, 64), 64)
    cols = pl.ds(pl.multiple_of(y * 1024, 1024), 1024)
    mine = pl.ds(pl.multiple_of(x * 64, 64), 64)
    pgb[mine, :] = (prompt[rows, :].astype(F32) * gain[...]).astype(BF16)

    def prompt_copy(d):
        return remote(pgb.at[mine, :], pgb.at[mine, :], p_snd.at[d], p_rcv.at[d], x_id(d))

    for d in (1, 2, 3):
        prompt_copy(d).start()
    steered = steer[...] * gain[...]
    high = steered.astype(BF16).astype(F32)
    which = lax.broadcasted_iota(jnp.int32, (16, D), 0)
    pgb[256:272, :] = jnp.where(which == 0, high, jnp.where(which == 1, steered - high, 0.0)).astype(BF16)

    qb[y] = jnp.zeros((4, 8, 256), F32)
    held(0, 0, columns_own().wait)
    for d in (1, 2, 3):
        held(0, 0, columns_copy(d).wait_recv)
    for h in (0, 1):
        ring_send(0, h, 1)
    for h in (0, 1):
        sibling_send(0, h, 0)
    load[2].wait()
    for p in (1, 2):
        for h in (0, 1):
            sibling_send(p, h, 0)

    for d, b in others:
        strengths_copy(d, b).wait()
    lane = lax.broadcasted_iota(jnp.int32, (64, 128), 1)
    table = jnp.zeros((64, 128), F32)
    by_row[0] = jnp.transpose(ids[...].astype(F32))
    by_row[1] = jnp.transpose(gates[...])
    name = by_row[0, rows, :].astype(jnp.int32)
    weight = by_row[1, rows, :]
    for k in range(8):
        table = table + jnp.where(lane == name[:, k:k + 1], weight[:, k:k + 1], 0.0)
    misc[x] = table

    @pl.loop(0, 8)
    def _(j):
        s = sbuf[j][0:1, 0:1]
        square = jnp.zeros((64, 128), F32)
        for n in range(32):
            here = slice(n * 128, (n + 1) * 128)
            piece = prompt[rows, here].astype(F32) + s * steer[:, here]
            square = square + piece * piece
        mean = jnp.sum(square, axis=1, keepdims=True) * (1.0 / D)
        misc[x] = misc[x] + jnp.where(lane == 16 + j, lax.rsqrt(mean + epsilon), 0.0)

    def misc_copy(d):
        return remote(misc.at[x], misc.at[x], m_snd.at[d], m_rcv.at[d], x_id(d))

    for d in (1, 2, 3):
        misc_copy(d).start()
    ring_take(0, 1)

    def turn(i):
        return lax.rem(zl + TURN[i], 4)

    def expert(i):
        e = turn(i)
        b = column(y, e)

        @pl.when(b < 3)
        def _():
            for n in ((3, 4), (2, 5), (1, 6), (0, 7))[i]:
                for h in (0, 1):
                    sibling(0, h, n).wait_recv()
            upper = jnp.dot(pgb[...], ub[e].reshape(D, 256), preferred_element_type=F32)
            here = pl.ds(pl.multiple_of(b * 256, 256), 256)
            for block in range(4):
                ab[block, e, :, here] = upper[block * 64:(block + 1) * 64].astype(BF16)
            qb[y, e] = upper[256:257] + upper[257:258] + jnp.zeros((8, 256), F32)
            for d in (1, 3):
                gather_copy(i, d).start()

    def owner(d):
        return y + (0 if d in (1, 3) else 3 if d == 2 else 1)

    def gather_copy(i, d):
        e = turn(i)
        here = pl.ds(pl.multiple_of(lax.rem(column(owner(d), e), 3) * 256, 256), 256)
        blocks = pl.ds(0, 4) if d in (1, 3) else pl.ds(0, 2) if d == 2 else pl.ds(2, 2)
        piece = ab.at[blocks, e, :, here]
        return remote(piece, piece, ag_snd.at[i, d], ag_rcv.at[i, d], yc_id((3, 1, 1, 3)[d], 0))

    def sent(i, d, fn):
        pl.when(column(owner(d), turn(i)) < 3)(fn)

    def came(i, d, fn):
        pl.when(column(y + (2, 3, 2, 1)[d], turn(i)) < 3)(fn)

    def forward(i):
        came(i, 1, gather_copy(i, 1).wait_recv)
        sent(i, 2, gather_copy(i, 2).start)
        came(i, 3, gather_copy(i, 3).wait_recv)
        sent(i, 0, gather_copy(i, 0).start)

    def push_copy(d):
        return remote(qb.at[y], qb.at[y], q_snd.at[d], q_rcv.at[d], yc_id(d, 0))

    for d in (1, 2, 3):
        misc_copy(d).wait_recv()

    @pl.loop(0, 4)
    def _(block):
        here = misc[block]
        for e in range(4):
            column = jnp.sum(jnp.where(lane == e * 4 + x, here, 0.0), axis=1, keepdims=True)
            gt[block, e] = jnp.broadcast_to(column, (64, 128))
        for j in range(8):
            it[block, j] = jnp.broadcast_to(0.5 * here[:, 16 + j:17 + j], (64, 128))

    ring_take(0, 2)
    for d in (1, 2, 3):
        prompt_copy(d).wait_recv()
    expert(0)
    ring_take(0, 3)
    ring_take(1, 1)
    expert(1)
    expert(2)
    forward(0)
    ring_take(0, 4)
    expert(3)
    for d in (1, 2, 3):
        push_copy(d).start()
    ring_take(1, 2)
    forward(1)
    forward(2)
    ring_take(1, 3)
    for h in (0, 1):
        ring_send(2, h, 1)
    forward(3)
    ring_take(1, 4)
    for i in range(4):
        for d in (0, 2):
            came(i, d, gather_copy(i, d).wait_recv)
    for d in (1, 2, 3):
        push_copy(d).wait_recv()

    @pl.loop(0, 4)
    def _(e):
        for b in range(3):
            push = qb[lax.rem(e + b, 4), e]
            for j in range(8):
                sq[j, e, :, b * 256:(b + 1) * 256] = push * sbuf[j][:, 0:1]

    def hidden(g):
        dest_y = lax.rem(y + g + 1, 4)

        @pl.loop(0, 16)
        def _(n):
            block, e = n // 4, lax.rem(n, 4)
            gate = gt[block, e]
            for b in range(2):
                j = dest_y * 2 + b
                inv = it[block, j]
                for m in range(6):
                    here = slice(m * 128, (m + 1) * 128)
                    pre = ab[block, e, :, here].astype(F32).reshape(8, 8, 128) + sq[j, e, :, here][None]
                    half = pre.reshape(64, 128) * inv
                    value = (half * gate) * (1.0 + jnp.tanh(half))
                    hb[g, pl.ds(pl.multiple_of(block * 128 + b * 64, 64), 64),
                       pl.ds(pl.multiple_of(e * EH + m * 128, 128), 128)] = value.astype(BF16)

    def passed(p):
        for h in (0, 1):
            for n in range(8):
                sibling(p, h, n).wait_recv()

    def relay(u, way):
        return remote(
            rsend.at[u, way], rrecv.at[u, way], rl_snd.at[u, way], rl_rcv.at[u, way], x_id(1 + 2 * way)
        )

    def main(u, way):
        return remote(
            msend.at[u, way], mrecv.at[u, way], mn_snd.at[u, way], mn_rcv.at[u, way], x_id(1 + 2 * way)
        )

    def final(g, b):
        return remote(
            fin.at[g, pl.ds(pl.multiple_of(lax.rem(c + b, 2) * 64, 64), 64), :],
            out.at[0, rows, cols], f_snd.at[g, b], f_rcv.at[g, b], yc_id(g + 1, b),
        )

    def final_local():
        return pltpu.make_async_copy(fin.at[3, rows, :], out.at[0, rows, cols], f_loc)

    def multiply(u, half):
        g = lax.rem(u, 4)

        @pl.loop(0, 2)
        def _(way):
            sums = jnp.dot(hb[g], db[half, way], preferred_element_type=F32)
            place = pl.ds(pl.multiple_of(way * 256, 256), 256)
            for block in range(4):
                part[u, block, :, place] = sums[block * 128:(block + 1) * 128]
            rsend[u, way] = part[u, lax.rem(x + 2, 4), :, place].astype(BF16)
            relay(u, way).start()

    def pass_on(u):
        for way in (0, 1):
            relay(u, way).wait_recv()
            block = lax.rem(x + 1 + 2 * way, 4)
            same = slice(way * 256, way * 256 + 256)
            other = slice(256 - way * 256, 512 - way * 256)
            msend[u, way, :, same] = (part[u, block, :, same] + rrecv[u, way].astype(F32)).astype(BF16)
            msend[u, way, :, other] = part[u, block, :, other].astype(BF16)
            main(u, way).start()

    def finish(u, half):
        g = lax.rem(u, 4)
        main(u, 0).wait_recv()
        main(u, 1).wait_recv()
        for n in range(4):
            here = slice(n * 128, n * 128 + 128)
            fin[g, :, n * 256 + half * 128:n * 256 + half * 128 + 128] = (
                part[u, x, :, here] + mrecv[u, 0, :, here].astype(F32) + mrecv[u, 1, :, here].astype(F32)
            ).astype(BF16)

    ring_take(2, 1)
    hidden(0)
    passed(1)
    multiply(0, 0)
    ring_take(2, 2)
    hidden(1)
    multiply(1, 0)
    ring_take(2, 3)
    pass_on(0)
    hidden(2)
    ring_take(2, 4)
    multiply(2, 0)
    pass_on(1)
    finish(0, 0)
    hidden(3)
    multiply(3, 0)
    pass_on(2)
    finish(1, 0)
    passed(2)

    @pl.loop(4, 10)
    def _(t):
        @pl.when(t < 8)
        def _():
            multiply(t, 1)

        @pl.when(t < 9)
        def _():
            pass_on(t - 1)

        @pl.when(t < 6)
        def _():
            finish(t - 2, 0)

        @pl.when(t >= 6)
        def _():
            finish(t - 2, 1)
            g = t - 6
            final(g, 1).start()

            @pl.when(g < 3)
            def _():
                final(g, 0).start()

            @pl.when(g == 3)
            def _():
                final_local().start()

    for d in (1, 2, 3):
        prompt_copy(d).wait_send()
        misc_copy(d).wait_send()
        push_copy(d).wait_send()
        pl.when(column(y + d, zl) < 3)(columns_copy(d).wait_send)
    for i in range(4):
        for d in range(4):
            sent(i, d, gather_copy(i, d).wait_send)
    for p in range(3):
        for h in (0, 1):
            for k in (1, 2, 3, 4):
                for way in ways(h, k):
                    held(p, (k - 1) * (2 * way - 1), ring(p, h, way, k).wait_send)
            for n in range(8):
                held(p, sibling_step(n), sibling(p, h, n).wait_send)
    for u in range(8):
        for way in (0, 1):
            relay(u, way).wait_send()
            main(u, way).wait_send()
    for g in range(4):
        for b in (0, 1):
            if (g, b) != (3, 0):
                final(g, b).wait()
    final_local().wait()


def local(prompt, steer_vec, strengths, norm_gain, expert_ids, gate_values, up_weight, down_weight):
    vmem = pl.BlockSpec(memory_space=pltpu.VMEM)
    away = pl.BlockSpec(memory_space=pl.ANY)
    dma = pltpu.SemaphoreType.DMA
    return pl.pallas_call(
        kernel,
        out_shape=jax.ShapeDtypeStruct((1, 128, D), BF16),
        in_specs=[vmem, vmem, pl.BlockSpec(memory_space=pltpu.SMEM)] + [vmem] * 4 + [away],
        out_specs=away,
        scratch_shapes=[
            pltpu.VMEM((8, 8, 128), F32),
            pltpu.VMEM((2, 128, 8), F32),
            pltpu.VMEM((272, D), BF16),
            pltpu.VMEM((4, 64, 128), F32),
            pltpu.VMEM((4, 4, 64, 128), F32),
            pltpu.VMEM((4, 8, 64, 128), F32),
            pltpu.VMEM((8, 4, 8, EH), F32),
            pltpu.VMEM((4, 4, 2, 2, 256, 256), BF16),
            pltpu.VMEM((2, 2, 4 * EH, 256), BF16),
            pltpu.VMEM((4, 4, 64, EH), BF16),
            pltpu.VMEM((4, 4, 8, 256), F32),
            pltpu.VMEM((4, 512, 4 * EH), BF16),
            pltpu.VMEM((8, 4, 128, 512), F32),
            pltpu.VMEM((8, 2, 128, 256), BF16),
            pltpu.VMEM((8, 2, 128, 256), BF16),
            pltpu.VMEM((8, 2, 128, 512), BF16),
            pltpu.VMEM((8, 2, 128, 512), BF16),
            pltpu.VMEM((4, 128, 1024), BF16),
            dma((3,)),
            dma((8,)), dma((8,)),
            dma((4,)), dma((4,)),
            dma((4,)), dma((4,)),
            dma((3, 2, 2, 4)), dma((3, 2, 2, 4)),
            dma((3, 2, 8)), dma((3, 2, 8)),
            dma((4,)), dma((4,)), dma(()),
            dma((4, 4)), dma((4, 4)),
            dma((4,)), dma((4,)),
            dma((8, 2)), dma((8, 2)),
            dma((8, 2)), dma((8, 2)),
            dma((4, 2)), dma((4, 2)),
            dma(()),
        ],
        compiler_params=pltpu.CompilerParams(
            collective_id=0, has_side_effects=True, vmem_limit_bytes=60 * 1024 * 1024
        ),
        cost_estimate=pl.CostEstimate(flops=18_000_000_000, bytes_accessed=3_000_000, transcendentals=6_300_000),
    )(
        prompt,
        steer_vec[None],
        strengths,
        norm_gain[None],
        expert_ids.T,
        gate_values.T,
        up_weight[0],
        down_weight[0],
    )


def solution(mesh):
    fine = Mesh(mesh.devices.reshape(4, 2, 2, 4, 4), ("y", "zh", "c", "zl", "x"))
    return jax.shard_map(
        local,
        mesh=fine,
        in_specs=(
            P(EXPERT, None),
            P(),
            P(WIDE),
            P(),
            P(EXPERT, None),
            P(EXPERT, None),
            P(EXPERT, WIDE, None),
            P(EXPERT, None, WIDE),
        ),
        out_specs=P(WIDE, EXPERT, None),
        check_vma=False,
    )
```

time: 152 us -> 137 us (0.901)
  Pallas kernels: 145 us -> 134 us
  local copies, waits for them, and re-layouts: 4.43 us -> 2.29 us
    pallas_call x1, Pallas kernels: 145 us -> 134 us  [local(): pl.pallas_call(kernel, out_shape=jax.ShapeDtypeStruct((1, 128, D), BF16),...]
    unnamed x7 -> x1, local copies, waits for them, and re-layouts: 3.84 us -> 2.29 us
where the time goes in v3:
time: 137 us
  Pallas kernels  134 us (98%)
  local copies, waits for them, and re-layouts  2.29 us (2%)
    pallas_call x1, Pallas kernels, local(): pl.pallas_call(kernel, out_shape=jax.ShapeDtypeStruct((1, 128, D), BF16),...  134 us

profile of v3, /device:TPU:16, one launch (start us, length us, event | category | flops | bytes accessed | tf_op | source)
XLA Modules:
  0.0 136.5 jit_solution(13360835345464647213)
XLA Ops:
  0.7 133.6 %shard_map.82 = bf16[1,128,4096]{2,1,0:T(8,128)(2,1)} custom-call(bf16[128,4096]{1,0:T(8,128)(2,1)} %prompt.1, f32[1,4096]{1,0:T(1,128)} %bitcast.8, f32[1]{0:T(128)S(6)} %copy.10.strength, f32[1,4096]{1,0:T(1,128)} %bitcast.9, s32[8,128]{1,0:T(8,128)} %bitcast.10, f32[8,128]{1,0:T(8,128)} %bitcast.11, bf16[256,768]{1,0:T(8,128)(2,1)} %bitcast.6, ...), custom_call_target="tpu_custom_call" | custom-call | flops 17999998976 | bytes 3000000 | tf_op jit(solution)/shard_map/pallas_call | solution.py:448
  134.2 2.3 %copy.11 = bf16[1,128,4096]{2,1,0:T(8,128)(2,1)} copy(bf16[1,128,4096]{2,1,0:T(8,128)(2,1)} %shard_map.82) | data formatting | bytes 2097152

commit v4 on v3

--- a/solution.py
+++ b/solution.py
@@ -159,18 +159,16 @@
     which = lax.broadcasted_iota(jnp.int32, (16, D), 0)
     pgb[256:272, :] = jnp.where(which == 0, high, jnp.where(which == 1, steered - high, 0.0)).astype(BF16)
 
-    qb[y] = jnp.zeros((4, 8, 256), F32)
-    held(0, 0, columns_own().wait)
-    for d in (1, 2, 3):
-        held(0, 0, columns_copy(d).wait_recv)
-    for h in (0, 1):
-        ring_send(0, h, 1)
-    for h in (0, 1):
-        sibling_send(0, h, 0)
     load[2].wait()
     for p in (1, 2):
         for h in (0, 1):
             sibling_send(p, h, 0)
+    held(0, 0, columns_own().wait)
+    for d in (1, 2, 3):
+        held(0, 0, columns_copy(d).wait_recv)
+    ring_send(0, 0, 1)
+    for h in (0, 1):
+        sibling_send(0, h, 0)
 
     for d, b in others:
         strengths_copy(d, b).wait()
@@ -200,6 +198,9 @@
 
     for d in (1, 2, 3):
         misc_copy(d).start()
+    for way in (0, 1):
+        held(0, 0, ring(0, 0, way, 1).wait_send)
+    ring_send(0, 1, 1)
     ring_take(0, 1)
 
     def turn(i):
@@ -221,6 +222,8 @@
             qb[y, e] = upper[256:257] + upper[257:258] + jnp.zeros((8, 256), F32)
             for d in (1, 3):
                 gather_copy(i, d).start()
+            for d in (1, 2, 3):
+                push_copy(i, d).start()
 
     def owner(d):
         return y + (0 if d in (1, 3) else 3 if d == 2 else 1)
@@ -244,8 +247,9 @@
         came(i, 3, gather_copy(i, 3).wait_recv)
         sent(i, 0, gather_copy(i, 0).start)
 
-    def push_copy(d):
-        return remote(qb.at[y], qb.at[y], q_snd.at[d], q_rcv.at[d], yc_id(d, 0))
+    def push_copy(i, d):
+        piece = qb.at[y, turn(i)]
+        return remote(piece, piece, q_snd.at[i, d], q_rcv.at[i, d], yc_id(d, 0))
 
     for d in (1, 2, 3):
         misc_copy(d).wait_recv()
@@ -259,49 +263,23 @@
         for j in range(8):
             it[block, j] = jnp.broadcast_to(0.5 * here[:, 16 + j:17 + j], (64, 128))
 
-    ring_take(0, 2)
-    for d in (1, 2, 3):
-        prompt_copy(d).wait_recv()
-    expert(0)
-    ring_take(0, 3)
-    ring_take(1, 1)
-    expert(1)
-    expert(2)
-    forward(0)
-    ring_take(0, 4)
-    expert(3)
-    for d in (1, 2, 3):
-        push_copy(d).start()
-    ring_take(1, 2)
-    forward(1)
-    forward(2)
-    ring_take(1, 3)
-    for h in (0, 1):
-        ring_send(2, h, 1)
-    forward(3)
-    ring_take(1, 4)
-    for i in range(4):
+    def gathered(i):
+        e = turn(i)
         for d in (0, 2):
             came(i, d, gather_copy(i, d).wait_recv)
-    for d in (1, 2, 3):
-        push_copy(d).wait_recv()
-
-    @pl.loop(0, 4)
-    def _(e):
+        for d in (1, 2, 3):
+            pl.when(column(y + 4 - d, e) < 3)(push_copy(i, d).wait_recv)
         for b in range(3):
             push = qb[lax.rem(e + b, 4), e]
             for j in range(8):
                 sq[j, e, :, b * 256:(b + 1) * 256] = push * sbuf[j][:, 0:1]
 
-    def hidden(g):
-        dest_y = lax.rem(y + g + 1, 4)
-
         @pl.loop(0, 16)
         def _(n):
-            block, e = n // 4, lax.rem(n, 4)
+            block, g = n // 4, lax.rem(n, 4)
             gate = gt[block, e]
             for b in range(2):
-                j = dest_y * 2 + b
+                j = lax.rem(y + g + 1, 4) * 2 + b
                 inv = it[block, j]
                 for m in range(6):
                     here = slice(m * 128, (m + 1) * 128)
@@ -310,6 +288,32 @@
                     value = (half * gate) * (1.0 + jnp.tanh(half))
                     hb[g, pl.ds(pl.multiple_of(block * 128 + b * 64, 64), 64),
                        pl.ds(pl.multiple_of(e * EH + m * 128, 128), 128)] = value.astype(BF16)
+
+    ring_take(0, 2)
+    ring_take(1, 1)
+    for d in (1, 2, 3):
+        prompt_copy(d).wait_recv()
+    expert(0)
+    ring_take(0, 3)
+    ring_take(1, 2)
+    expert(1)
+    expert(2)
+    forward(0)
+    ring_take(0, 4)
+    expert(3)
+    ring_take(1, 3)
+    for h in (0, 1):
+        ring_send(2, h, 1)
+    forward(1)
+    forward(2)
+    gathered(0)
+    forward(3)
+    ring_take(1, 4)
+    gathered(1)
+    ring_take(2, 1)
+    gathered(2)
+    gathered(3)
+    ring_take(2, 2)
 
     def passed(p):
         for h in (0, 1):
@@ -367,24 +371,19 @@
                 part[u, x, :, here] + mrecv[u, 0, :, here].astype(F32) + mrecv[u, 1, :, here].astype(F32)
             ).astype(BF16)
 
-    ring_take(2, 1)
-    hidden(0)
     passed(1)
     multiply(0, 0)
-    ring_take(2, 2)
-    hidden(1)
+    ring_take(2, 3)
     multiply(1, 0)
-    ring_take(2, 3)
     pass_on(0)
-    hidden(2)
     ring_take(2, 4)
-    multiply(2, 0)
-    pass_on(1)
-    finish(0, 0)
-    hidden(3)
-    multiply(3, 0)
-    pass_on(2)
-    finish(1, 0)
+
+    @pl.loop(2, 4)
+    def _(t):
+        multiply(t, 0)
+        pass_on(t - 1)
+        finish(t - 2, 0)
+
     passed(2)
 
     @pl.loop(4, 10)
@@ -418,16 +417,18 @@
     for d in (1, 2, 3):
         prompt_copy(d).wait_send()
         misc_copy(d).wait_send()
-        push_copy(d).wait_send()
         pl.when(column(y + d, zl) < 3)(columns_copy(d).wait_send)
     for i in range(4):
+        for d in (1, 2, 3):
+            sent(i, 1, push_copy(i, d).wait_send)
         for d in range(4):
             sent(i, d, gather_copy(i, d).wait_send)
     for p in range(3):
         for h in (0, 1):
             for k in (1, 2, 3, 4):
                 for way in ways(h, k):
-                    held(p, (k - 1) * (2 * way - 1), ring(p, h, way, k).wait_send)
+                    if (p, h, k) != (0, 0, 1):
+                        held(p, (k - 1) * (2 * way - 1), ring(p, h, way, k).wait_send)
             for n in range(8):
                 held(p, sibling_step(n), sibling(p, h, n).wait_send)
     for u in range(8):
@@ -477,7 +478,7 @@
             dma((3, 2, 8)), dma((3, 2, 8)),
             dma((4,)), dma((4,)), dma(()),
             dma((4, 4)), dma((4, 4)),
-            dma((4,)), dma((4,)),
+            dma((4, 4)), dma((4, 4)),
             dma((8, 2)), dma((8, 2)),
             dma((8, 2)), dma((8, 2)),
             dma((4, 2)), dma((4, 2)),

time: 137 us -> 133 us (0.971); the launches traced: 137 us -> 130 us
  Pallas kernels: 134 us -> 127 us
    pallas_call x1, Pallas kernels: 134 us -> 127 us  [local(): pl.pallas_call(kernel, out_shape=jax.ShapeDtypeStruct((1, 128, D), BF16),...]
where the time goes in v4:
time: 133 us; the launch traced here: 130 us
  Pallas kernels  127 us (95%)
  local copies, waits for them, and re-layouts  2.29 us (2%)
    pallas_call x1, Pallas kernels, local(): pl.pallas_call(kernel, out_shape=jax.ShapeDtypeStruct((1, 128, D), BF16),...  127 us

profile of v4, /device:TPU:16, one launch (start us, length us, event | category | flops | bytes accessed | tf_op | source)
XLA Modules:
  0.0 130.4 jit_solution(8542820076441192650)
XLA Ops:
  0.7 127.5 %shard_map.82 = bf16[1,128,4096]{2,1,0:T(8,128)(2,1)} custom-call(bf16[128,4096]{1,0:T(8,128)(2,1)} %prompt.1, f32[1,4096]{1,0:T(1,128)} %bitcast.8, f32[1]{0:T(128)S(6)} %copy.10.strength, f32[1,4096]{1,0:T(1,128)} %bitcast.9, s32[8,128]{1,0:T(8,128)} %bitcast.10, f32[8,128]{1,0:T(8,128)} %bitcast.11, bf16[256,768]{1,0:T(8,128)(2,1)} %bitcast.6, ...), custom_call_target="tpu_custom_call" | custom-call | flops 17999998976 | bytes 3000000 | tf_op jit(solution)/shard_map/pallas_call | solution.py:449
  128.1 2.3 %copy.11 = bf16[1,128,4096]{2,1,0:T(8,128)(2,1)} copy(bf16[1,128,4096]{2,1,0:T(8,128)(2,1)} %shard_map.82) | data formatting | bytes 2097152

commit v5 on v4

--- a/solution.py
+++ b/solution.py
@@ -130,8 +130,6 @@
     for d in (1, 2, 3):
         pl.when(column(y + d, zl) < 3)(columns_copy(d).start)
     load[1].wait()
-    for h in (0, 1):
-        ring_send(1, h, 1)
 
     me = y * 2 + c
     sbuf[me] = jnp.full((8, 128), strength[0], F32)
@@ -202,6 +200,8 @@
         held(0, 0, ring(0, 0, way, 1).wait_send)
     ring_send(0, 1, 1)
     ring_take(0, 1)
+    for h in (0, 1):
+        ring_send(1, h, 1)
 
     def turn(i):
         return lax.rem(zl + TURN[i], 4)
@@ -313,7 +313,6 @@
     ring_take(2, 1)
     gathered(2)
     gathered(3)
-    ring_take(2, 2)
 
     def passed(p):
         for h in (0, 1):
@@ -373,16 +372,17 @@
 
     passed(1)
     multiply(0, 0)
-    ring_take(2, 3)
+    ring_take(2, 2)
     multiply(1, 0)
     pass_on(0)
+    ring_take(2, 3)
+    multiply(2, 0)
+    pass_on(1)
+    finish(0, 0)
     ring_take(2, 4)
-
-    @pl.loop(2, 4)
-    def _(t):
-        multiply(t, 0)
-        pass_on(t - 1)
-        finish(t - 2, 0)
+    multiply(3, 0)
+    pass_on(2)
+    finish(1, 0)
 
     passed(2)
 

time: 133 us -> 135 us (1.015)
  Pallas kernels: 127 us -> 130 us
    pallas_call x1, Pallas kernels: 127 us -> 130 us  [local(): pl.pallas_call(kernel, out_shape=jax.ShapeDtypeStruct((1, 128, D), BF16),...]
where the time goes in v5:
time: 135 us; the launch traced here: 133 us
  Pallas kernels  130 us (96%)
  local copies, waits for them, and re-layouts  2.29 us (2%)
    pallas_call x1, Pallas kernels, local(): pl.pallas_call(kernel, out_shape=jax.ShapeDtypeStruct((1, 128, D), BF16),...  130 us

profile of v5, /device:TPU:16, one launch (start us, length us, event | category | flops | bytes accessed | tf_op | source)
XLA Modules:
  0.0 132.6 jit_solution(10513512647002001857)
XLA Ops:
  0.7 129.7 %shard_map.82 = bf16[1,128,4096]{2,1,0:T(8,128)(2,1)} custom-call(bf16[128,4096]{1,0:T(8,128)(2,1)} %prompt.1, f32[1,4096]{1,0:T(1,128)} %bitcast.8, f32[1]{0:T(128)S(6)} %copy.10.strength, f32[1,4096]{1,0:T(1,128)} %bitcast.9, s32[8,128]{1,0:T(8,128)} %bitcast.10, f32[8,128]{1,0:T(8,128)} %bitcast.11, bf16[256,768]{1,0:T(8,128)(2,1)} %bitcast.6, ...), custom_call_target="tpu_custom_call" | custom-call | flops 17999998976 | bytes 3000000 | tf_op jit(solution)/shard_map/pallas_call | solution.py:449
  130.3 2.3 %copy.11 = bf16[1,128,4096]{2,1,0:T(8,128)(2,1)} copy(bf16[1,128,4096]{2,1,0:T(8,128)(2,1)} %shard_map.82) | data formatting | bytes 2097152
